TPU v7x, 32 devices: a whole 2x2x4 slice. The times are simulated.
32 devices in a mesh: dp: 2 (over core), row: 4 (over y, x), col: 4 (over z).
Axes of the slice: x: 2, y: 2, z: 4, core: 2. Of those that a mesh axis runs over, the one named last changes fastest.
Arguments:
- forget_tokens: bfloat16 [256, 6144], P('dp', 'col'), may hold values from -6 to 6
- forget_cotangent: bfloat16 [256, 6144], P('dp', 'col'), may hold values from -6 to 6
- forget_labels: int32 [256], P('dp'), may hold values 0 or 1
- retain_tokens: bfloat16 [256, 6144], P('dp', 'col'), may hold values from -6 to 6
- ln_gain: float32 [6144], P('col'), may hold values from 0.25 to 1.75
- w_in: bfloat16 [6144, 24576], P('col', 'row'), may hold values from -0.078125 to 0.078125
- b_in: float32 [24576], P('row'), may hold values from -3 to 3
- w_out: bfloat16 [24576, 6144], P('row', 'col'), may hold values from -0.0390625 to 0.0390625
- b_out: float32 [6144], P('col'), may hold values from -3 to 3
- pruned: int32 [512], P('row'), may hold values from 0 to 24575, as said below
Outputs:
- saliency: float32 [24576], P('row')
- retain_out: bfloat16 [256, 6144], P(('dp', 'row'), 'col')
Inputs may be any that keep to these rules, and one draw needn't show every extreme that they name: `pruned`: entries r * 128 to (r + 1) * 128 - 1 are distinct neurons that all lie in the r-th of the equal neuron ranges of the row shards.
All inputs are finite; a program needn't handle non-finite values. No bound on the sum of `forget_labels` on one device may be relied on, other than what follows from the above.
Results may differ from a plain program's by a relative error of at most 0.0052.
Values may be sent and summed in bfloat16 or wider, within the bound.
A program may use at most 256 MiB of HBM per device.

v0:
```python
import jax
import jax.numpy as jnp
from jax import lax
from jax.sharding import PartitionSpec as P

D = 6144


def gelu_exact(v):
    return v * 0.5 * (1.0 + lax.erf(v * 0.7071067811865476))


def gelu_slope(v):
    return (
        0.5 * (1.0 + lax.erf(v * 0.7071067811865476))
        + v * jnp.exp(-0.5 * v * v) * 0.3989422804014327
    )


def outer_rows(left, right):
    return lax.dot_general(
        left, right, (((0,), (0,)), ((), ())), preferred_element_type=jnp.float32
    )


def local(
    forget_tokens,
    forget_cotangent,
    forget_labels,
    retain_tokens,
    ln_gain,
    w_in,
    b_in,
    w_out,
    b_out,
    pruned,
):
    forget_rows = forget_tokens.shape[0]
    width_local = w_in.shape[0]
    neurons_local = w_in.shape[1]
    joined = jnp.concatenate([forget_tokens, retain_tokens], axis=0).astype(jnp.float32)
    mean_val = lax.psum(jnp.sum(joined, axis=1, keepdims=True), "col") / D
    centred = joined - mean_val
    var_val = lax.psum(jnp.sum(centred * centred, axis=1, keepdims=True), "col") / D
    normed = (centred * lax.rsqrt(var_val + 1e-06) * ln_gain).astype(jnp.bfloat16)
    partial_pre = jnp.dot(normed, w_in, preferred_element_type=jnp.float32)
    grad_y = forget_cotangent * forget_labels[:, None].astype(jnp.bfloat16)
    grad_part = lax.dot_general(
        grad_y, w_out, (((1,), (1,)), ((), ())), preferred_element_type=jnp.float32
    )
    share_width = neurons_local // lax.axis_size("col")
    share_start = lax.axis_index("col") * share_width
    bias_share = lax.dynamic_slice_in_dim(b_in, share_start, share_width, 0)
    pre_share = lax.psum_scatter(partial_pre, "col", scatter_dimension=1, tiled=True) + bias_share
    act_share = gelu_exact(pre_share).astype(jnp.bfloat16)
    act_all = lax.all_gather(act_share, "col", axis=1, tiled=True)
    grad_act_share = lax.psum_scatter(
        grad_part.astype(jnp.bfloat16), "col", scatter_dimension=1, tiled=True
    ).astype(jnp.float32)
    grad_pre_share = (grad_act_share * gelu_slope(pre_share[:forget_rows])).astype(jnp.bfloat16)
    grad_pre = lax.all_gather(grad_pre_share, "col", axis=1, tiled=True)
    act_f = act_all[:forget_rows]
    act_r = act_all[forget_rows:]
    normed_f = normed[:forget_rows]
    local_in = outer_rows(normed_f, grad_pre)
    local_out = outer_rows(act_f, grad_y)
    summed_in, summed_out = (
        lax.psum_scatter(
            local_in.astype(jnp.bfloat16), "dp", scatter_dimension=0, tiled=True
        ).astype(jnp.float32),
        lax.psum_scatter(
            local_out.astype(jnp.bfloat16), "dp", scatter_dimension=1, tiled=True
        ).astype(jnp.float32),
    )
    slice_rows = width_local // lax.axis_size("dp")
    slice_start = lax.axis_index("dp") * slice_rows
    weight_in_rows = lax.dynamic_slice_in_dim(w_in, slice_start, slice_rows, 0).astype(jnp.float32)
    weight_out_cols = lax.dynamic_slice_in_dim(w_out, slice_start, slice_rows, 1).astype(
        jnp.float32
    )
    terms = jnp.sum(jnp.abs(weight_in_rows * summed_in), axis=0) + jnp.sum(
        jnp.abs(weight_out_cols * summed_out), axis=1
    )
    saliency = lax.psum(terms, ("dp", "col")) / D
    neuron_ids = lax.axis_index("row") * neurons_local + jnp.arange(neurons_local, dtype=jnp.int32)
    is_pruned = jnp.any(pruned[:, None] == neuron_ids[None, :], axis=0)
    keep = jnp.where(is_pruned, 0.0, 1.0).astype(jnp.bfloat16)
    masked_r = act_r * keep[None, :]
    out_part = jnp.dot(masked_r, w_out, preferred_element_type=jnp.float32)
    retain_out = (
        lax.psum_scatter(out_part, "row", scatter_dimension=0, tiled=True) + b_out
    ).astype(jnp.bfloat16)
    return (saliency, retain_out)


def solution(mesh):
    in_specs = (
        P("dp", "col"),
        P("dp", "col"),
        P("dp"),
        P("dp", "col"),
        P("col"),
        P("col", "row"),
        P("row"),
        P("row", "col"),
        P("col"),
        P("row"),
    )
    out_specs = (P("row"), P(("dp", "row"), "col"))
    return jax.shard_map(local, mesh=mesh, in_specs=in_specs, out_specs=out_specs, check_vma=False)
```

profile of v0, /device:TPU:0, one launch (start us, length us, event | category | flops | bytes accessed | tf_op | source)
XLA Modules:
  0.0 432.1 jit_solution(5603609527668077118)
XLA Ops:
  7.2 1.4 convert_reduce_fusion
  8.6 13.5 %psum.21 = f32[256,1]{0,1:T(1,128)S(1)} all-reduce(f32[256,1]{0,1:T(1,128)S(1)} %bitcast.12), channel_id=1, replica_groups=mesh['dp'=2,'row'=4,'col'=4] {'col'}, use_global_device_ids=true, to_apply=%region_1.0 | all-reduce | flops 256 | bytes 2048 | tf_op jit(solution)/shard_map/psum | solution.py:42
  22.1 1.5 fusion.2
  23.5 8.4 %psum.22 = f32[256,1]{0,1:T(1,128)S(1)} all-reduce(f32[256,1]{0,1:T(1,128)S(1)} %bitcast.13), channel_id=1, replica_groups=mesh['dp'=2,'row'=4,'col'=4] {'col'}, use_global_device_ids=true, to_apply=%region_3.0 | all-reduce | flops 256 | bytes 2048 | tf_op jit(solution)/shard_map/psum | solution.py:44
  31.9 0.3 fusion.4
  32.2 13.3 %fusion.19 = f32[256,6144]{1,0:T(8,128)} fusion(bf16[256,1536]{1,0:T(8,128)(2,1)S(1)} %fusion.4, bf16[1536,6144]{1,0:T(8,128)(2,1)} %param.15), kind=kOutput, calls=%fused_computation.38 | convolution fusion | flops 4831838208 | bytes 25952256 | tf_op jit(solution)/shard_map/dot_general | solution.py:46
  45.6 0.0 reduce-scatter.6.cloned.1.call-start
  45.7 0.6 copy-done.7
  46.2 0.4 copy-done.3
  46.6 14.9 %convolution_convert_fusion.2 = bf16[128,6144]{1,0:T(8,128)(2,1)} fusion(bf16[6144,1536]{1,0:T(8,128)(2,1)} %param.17, bf16[128,1536]{1,0:T(8,128)(2,1)S(1)} %copy-done.3, bf16[128]{0:T(256)(128)(2,1)S(1)} %convert_element_type.53), kind=kOutput, calls=%fused_computation.4 | convolution fusion | flops 2416902144 | bytes 20840704 | tf_op jit(solution)/shard_map/dot_general | solution.py:48
  61.6 0.8 dynamic_slice.10
  62.3 93.8 %reduce-scatter.8.cloned.1.call-done = f32[256,1536]{1,0:T(8,128)} async-done(((f32[256,6144]{1,0:T(8,128)}), f32[256,1536]{1,0:T(8,128)}) %reduce-scatter.8.cloned.1.call-update) | async-done | bytes 1572880 | tf_op jit(solution)/shard_map/reduce_scatter | solution.py:54
  156.2 2.6 multiply_convert_fusion
  158.9 35.4 %reduce-scatter.6.cloned.1.call-done = bf16[128,1536]{1,0:T(8,128)(2,1)} async-done(((bf16[128,6144]{1,0:T(8,128)(2,1)}), bf16[128,1536]{1,0:T(8,128)(2,1)}) %reduce-scatter.6.cloned.1.call-update) | async-done | bytes 393232 | tf_op jit(solution)/shard_map/reduce_scatter | solution.py:57
  194.3 2.1 fusion.12
  196.5 0.5 compare_reduce_fusion
  197.0 61.3 %all-gather.5.cloned.1.call-done = bf16[256,6144]{1,0:T(8,128)(2,1)} async-done(((bf16[256,1536]{1,0:T(8,128)(2,1)}), bf16[256,6144]{1,0:T(8,128)(2,1)}) %all-gather.5.cloned.1.call-update) | async-done | bytes 3145744 | tf_op jit(solution)/shard_map/all_gather | solution.py:56
  258.4 10.4 %fusion.5 = f32[128,1536]{1,0:T(8,128)} fusion(bf16[6144,1536]{1,0:T(8,128)(2,1)} %param.17, bf16[256,6144]{1,0:T(8,128)(2,1)} %all-gather.5.cloned.1.call-done, bf16[6144]{0:T(1024)(128)(2,1)S(1)} %select_convert_fusion), kind=kOutput, calls=%fused_computation.14 | convolution fusion | flops 2416705536 | bytes 21245952 | tf_op jit(solution)/shard_map/dot_general | solution.py:89
  268.8 0.2 reduce-scatter.10.cloned.1.call-start
  269.1 26.5 %all-gather.3.cloned.1.call-done = bf16[128,6144]{1,0:T(8,128)(2,1)} async-done(((bf16[128,1536]{1,0:T(8,128)(2,1)}), bf16[128,6144]{1,0:T(8,128)(2,1)}) %all-gather.3.cloned.1.call-update) | async-done | bytes 1572880 | tf_op jit(solution)/shard_map/all_gather | solution.py:61
  295.6 10.7 %convolution_convert_fusion.1 = bf16[1536,6144]{1,0:T(8,128)(2,1)} fusion(bf16[128,6144]{1,0:T(8,128)(2,1)} %all-gather.3.cloned.1.call-done, bf16[256,1536]{1,0:T(8,128)(2,1)S(1)} %fusion.4), kind=kOutput, calls=%fused_computation.1 | convolution fusion | flops 2425356288 | bytes 20840448 | tf_op jit(solution)/shard_map/dot_general | solution.py:21
  306.3 0.0 reduce-scatter.12.cloned.1.call-start
  306.3 1.9 copy-done
  308.2 9.1 %convolution_convert_fusion = bf16[6144,1536]{1,0:T(8,128)(2,1)} fusion(bf16[256,6144]{1,0:T(8,128)(2,1)S(1)} %copy-done, bf16[128,1536]{1,0:T(8,128)(2,1)S(1)} %copy-done.3, bf16[128]{0:T(256)(128)(2,1)S(1)} %convert_element_type.53), kind=kOutput, calls=%fused_computation | convolution fusion | flops 2425552896 | bytes 20840960 | tf_op jit(solution)/shard_map/dot_general | solution.py:21
  317.4 6.0 %reduce-scatter.14.cloned.1.call-done = f32[32,1536]{1,0:T(8,128)} async-done(((f32[128,1536]{1,0:T(8,128)}), f32[32,1536]{1,0:T(8,128)}) %reduce-scatter.14.cloned.1.call-update) | async-done | bytes 196624 | tf_op jit(solution)/shard_map/reduce_scatter | solution.py:91
  323.3 1.6 add_convert_fusion
  324.9 28.9 %reduce-scatter.10.cloned.1.call-done = bf16[768,6144]{1,0:T(8,128)(2,1)} async-done(((bf16[1536,6144]{1,0:T(8,128)(2,1)}), bf16[768,6144]{1,0:T(8,128)(2,1)}) %reduce-scatter.10.cloned.1.call-update) | async-done | bytes 9437200 | tf_op jit(solution)/shard_map/reduce_scatter | solution.py:68
  353.8 10.5 %abs_reduce_fusion.1 = f32[6144]{0:T(1024)S(1)} fusion(bf16[768,6144]{1,0:T(8,128)(2,1)} %reduce-scatter.10.cloned.1.call-done, bf16[1536,6144]{1,0:T(8,128)(2,1)} %param.15, s32[]{:T(128)S(6)} %select_n.15), kind=kLoop, calls=%fused_computation.3 | loop fusion | flops 23586816 | bytes 18898948 | tf_op jit(solution)/shard_map/reduce_sum | solution.py:81
  364.3 21.4 %reduce-scatter.12.cloned.1.call-done = bf16[6144,768]{1,0:T(8,128)(2,1)} async-done(((bf16[6144,1536]{1,0:T(8,128)(2,1)}), bf16[6144,768]{1,0:T(8,128)(2,1)}) %reduce-scatter.12.cloned.1.call-update) | async-done | bytes 9437200 | tf_op jit(solution)/shard_map/reduce_scatter | solution.py:71
  385.7 9.5 %abs_reduce_fusion = f32[6144]{0:T(1024)S(1)} fusion(bf16[6144,768]{1,0:T(8,128)(2,1)} %reduce-scatter.12.cloned.1.call-done, bf16[6144,1536]{1,0:T(8,128)(2,1)} %param.17, s32[]{:T(128)S(6)} %select_n.15), kind=kLoop, calls=%fused_computation.2 | loop fusion | flops 23586816 | bytes 18898948 | tf_op jit(solution)/shard_map/reduce_sum | solution.py:81
  395.2 29.5 %psum.23 = f32[6144]{0:T(1024)S(1)} all-reduce(f32[6144]{0:T(1024)S(1)} %add.84), channel_id=1, replica_groups=mesh['dp'=2,'row'=4,'col'=4] {'dp','col'}, use_global_device_ids=true, to_apply=%region_10.0 | all-reduce | flops 6144 | bytes 49152 | tf_op jit(solution)/shard_map/psum | solution.py:84
  424.6 0.6 broadcast_multiply_fusion
  (30 shorter events, 0.3 us)
Async XLA Ops:
  7.2 24.8 %copy-start.1 = (bf16[128,1536]{1,0:T(8,128)(2,1)S(1)}, bf16[128,1536]{1,0:T(8,128)(2,1)}, u32[]{:S(2)}) copy-start(bf16[128,1536]{1,0:T(8,128)(2,1)} %param.13) | copy-start | bytes 1179652
  7.2 24.7 %copy-start.2 = (bf16[128,1536]{1,0:T(8,128)(2,1)S(1)}, bf16[128,1536]{1,0:T(8,128)(2,1)}, u32[]{:S(2)}) copy-start(bf16[128,1536]{1,0:T(8,128)(2,1)} %param.10) | copy-start | bytes 1179652
  7.2 24.7 %copy-start.4 = (f32[1536]{0:T(1024)S(1)}, f32[1536]{0:T(1024)}, u32[]{:S(2)}) copy-start(f32[1536]{0:T(1024)} %param.14) | copy-start | bytes 18436
  7.2 149.0 %reduce-scatter.8.cloned.1.call-start = ((), (), s32[]{:S(2)}) async-start(), calls=%async_computation.6 | async-start | bytes 7864320 | tf_op jit(solution)/shard_map/reduce_scatter | solution.py:54
  45.6 0.7 copy-start.7
  45.6 1.0 copy-start.3
  45.6 148.7 %reduce-scatter.6.cloned.1.call-start = ((), (), s32[]{:S(2)}) async-start(), calls=%async_computation.5 | async-start | bytes 1966080 | tf_op jit(solution)/shard_map/reduce_scatter | solution.py:57
  61.5 196.9 %all-gather.5.cloned.1.call-start = ((), (), s32[]{:S(2)}) async-start(), calls=%async_computation.9 | async-start | bytes 3932160 | tf_op jit(solution)/shard_map/all_gather | solution.py:56
  158.8 37.7 %copy-start.6 = (s32[128]{0:T(128)S(1)}, s32[128]{0:T(128)}, u32[]{:S(2)}) copy-start(s32[128]{0:T(128)} %param.19) | copy-start | bytes 1540
  158.8 136.8 %all-gather.3.cloned.1.call-start = ((), (), s32[]{:S(2)}) async-start(), calls=%async_computation.7 | async-start | bytes 1966080 | tf_op jit(solution)/shard_map/all_gather | solution.py:61
  196.4 126.9 %reduce-scatter.14.cloned.1.call-start = ((), (), s32[]{:S(2)}) async-start(), calls=%async_computation.11 | async-start | bytes 983040 | tf_op jit(solution)/shard_map/reduce_scatter | solution.py:91
  268.8 84.9 %reduce-scatter.10.cloned.1.call-start = ((), (), s32[]{:S(2)}) async-start(), calls=%async_computation.8 | async-start | bytes 28311552 | tf_op jit(solution)/shard_map/reduce_scatter | solution.py:68
  306.3 1.9 copy-start
  306.3 79.4 %reduce-scatter.12.cloned.1.call-start = ((), (), s32[]{:S(2)}) async-start(), calls=%async_computation.10 | async-start | bytes 28311552 | tf_op jit(solution)/shard_map/reduce_scatter | solution.py:71
  317.3 6.0 %copy-start.5 = (f32[1536]{0:T(1024)S(1)}, f32[1536]{0:T(1024)}, u32[]{:S(2)}) copy-start(f32[1536]{0:T(1024)} %param.18) | copy-start | bytes 18436
Sparse Core Ops, SparseCore 0:
  45.7 110.3 reduce-scatter.7
  158.5 35.8 reduce-scatter.5
  195.9 62.4 all-gather.4
  259.8 35.7 all-gather.2
  298.3 24.9 reduce-scatter.13
  325.5 28.2 reduce-scatter.9
  356.1 29.5 reduce-scatter.11
where the time goes:
time: 433 us; the launch traced here: 432 us
  waiting for transfers between devices  273 us (63%)
  matrix products  58.5 us (14%)
  blocking collectives  51.3 us (12%)
  other arithmetic  30.6 us (7%)
  between operations  14.2 us (3%)
    reduce_scatter x1, waiting for transfers between devices, local(): lax.psum_scatter(partial_pre, 'col', scatter_dimension=1, tiled=True)  93.8 us
    all_gather x1, waiting for transfers between devices, local(): act_all = lax.all_gather(act_share, 'col', axis=1, tiled=True)  61.3 us
    reduce_scatter x1, waiting for transfers between devices, local(): lax.psum_scatter(grad_part.astype(jnp.bfloat16), 'col', scatter_dimension...  35.4 us
    psum x1, blocking collectives, local(): saliency = lax.psum(terms, ('dp', 'col')) / D  29.5 us
    reduce_scatter x1, waiting for transfers between devices, local(): lax.psum_scatter(local_in.astype(jnp.bfloat16), 'dp', scatter_dimension=0...  28.9 us
    all_gather x1, waiting for transfers between devices, local(): grad_pre = lax.all_gather(grad_pre_share, 'col', axis=1, tiled=True)  26.5 us
    reduce_scatter x1, waiting for transfers between devices, local(): lax.psum_scatter(local_out.astype(jnp.bfloat16), 'dp', scatter_dimension=...  21.4 us
    dot_general x2, matrix products, outer_rows(): lax.dot_general(left, right, (((0,), (0,)), ((), ())), preferred_element_...  19.8 us
  transfers between devices with their start and end apart: 7, of which 7 were waited for; matrix products, arithmetic and copies ran while one was open for 15% of the time, Pallas kernels for 0%

commit v1 on v0

v1 whole, which is shorter than its diff:
```python
import functools

import jax
import jax.numpy as jnp
from jax import lax
from jax.experimental import pallas as pl
from jax.experimental.pallas import tpu as pltpu
from jax.sharding import PartitionSpec as P

F32, BF16 = jnp.float32, jnp.bfloat16
MESH = pl.DeviceIdType.MESH
CHUNK = 256
LAG = 2


def dot(left, right, contract=((1,), (0,))):
    return lax.dot_general(left, right, (contract, ((), ())), preferred_element_type=F32)


def kernel(
    sizes,
    ft_hbm, rt_hbm, gy_hbm, win_hbm, wout_hbm, gain_ref, bin_ref, keep_ref, bout_ref,
    sal_out, ret_out,
    raw, gy, nrm, nrm_t, stats, win, wout, part, from_left, from_right, to_right, to_left,
    acc, half, blocks, mine, sal, sal_all, sal_fin,
    raw_loc, raw_send, raw_recv, st_send, st_recv, win_sem, wout_sem,
    right_send, right_recv, left_send, left_recv,
    half_send, half_recv, blk_send, blk_recv, sal_send, sal_recv, fin_send, fin_recv,
):
    cols, rows, tokens, nch = sizes
    width = nrm.shape[1]
    both = 2 * tokens
    dp, row, z = lax.axis_index("dp"), lax.axis_index("row"), lax.axis_index("col")
    other = 1 - dp

    def at_dp(d):
        return (d, row, z)

    def at_row(r):
        return (dp, r, z)

    def at_col(c):
        return (dp, row, c)

    def win_copy(c):
        lanes = pl.ds(pl.multiple_of((dp * nch + c) * CHUNK, CHUNK), CHUNK)
        return pltpu.make_async_copy(win_hbm.at[:, lanes], win.at[c], win_sem.at[c])

    def wout_copy(c):
        lines = pl.ds(pl.multiple_of((dp * nch + c) * CHUNK, CHUNK), CHUNK)
        return pltpu.make_async_copy(wout_hbm.at[lines, :], wout.at[c], wout_sem.at[c])

    sources = (ft_hbm, rt_hbm, gy_hbm)
    places = (raw.at[0, dp], raw.at[1, dp], gy.at[dp])
    own = [
        pltpu.make_async_copy(src, dst, raw_loc.at[i])
        for i, (src, dst) in enumerate(zip(sources, places))
    ]
    for copy in own:
        copy.start()

    @pl.loop(0, nch)
    def _(c):
        win_copy(c).start()
        wout_copy(c).start()

    barrier = pltpu.get_barrier_semaphore()
    pl.semaphore_signal(barrier, inc=1, device_id=at_dp(other), device_id_type=MESH)
    for o in range(1, cols):
        pl.semaphore_signal(
            barrier, inc=1, device_id=at_col(lax.rem(z + o, cols)), device_id_type=MESH
        )
    for o in range(1, rows):
        pl.semaphore_signal(
            barrier, inc=1, device_id=at_row(lax.rem(row + o, rows)), device_id_type=MESH
        )
    pl.semaphore_wait(barrier, 1 + (cols - 1) + (rows - 1))

    swaps = [
        pltpu.make_async_remote_copy(
            src_ref=src, dst_ref=dst, send_sem=raw_send.at[i], recv_sem=raw_recv.at[i],
            device_id=at_dp(other), device_id_type=MESH,
        )
        for i, (src, dst) in enumerate(zip(sources, places))
    ]
    for copy in swaps:
        copy.start()
    for copy in own:
        copy.wait()
    for copy in swaps:
        copy.wait()

    for kind in range(2):
        x = raw[kind].reshape(both, width).astype(F32)
        mean_here = jnp.sum(x, axis=1, keepdims=True) * (1.0 / width)
        cent = x - mean_here
        square = jnp.sum(cent * cent, axis=1, keepdims=True)
        lane = lax.broadcasted_iota(jnp.int32, (both, 128), 1)
        tile = jnp.where(lane == 0, mean_here, square)
        stats[z, :, kind * both : (kind + 1) * both] = jnp.transpose(tile)[0:8, :]
    stat_copies = [
        pltpu.make_async_remote_copy(
            src_ref=stats.at[z], dst_ref=stats.at[z],
            send_sem=st_send.at[o - 1], recv_sem=st_recv.at[o - 1],
            device_id=at_col(lax.rem(z + o, cols)), device_id_type=MESH,
        )
        for o in range(1, cols)
    ]
    for copy in stat_copies:
        copy.start()
    for copy in stat_copies:
        copy.wait()
    means = stats[:, 0:1, :]
    mean_all = jnp.sum(means, axis=0) * (1.0 / cols)
    spread = means - mean_all[None]
    squares = jnp.sum(stats[:, 1:2, :] + width * (spread * spread), axis=0)
    scale_all = lax.rsqrt(squares * (1.0 / (width * cols)) + 1e-06)
    for kind in range(2):
        lanes = slice(kind * both, (kind + 1) * both)
        line = lax.broadcasted_iota(jnp.int32, (128, both), 0)
        tile = jnp.transpose(jnp.where(line == 0, mean_all[:, lanes], scale_all[:, lanes]))
        x = raw[kind].reshape(both, width).astype(F32)
        normed = (x - tile[:, 0:1]) * tile[:, 1:2] * gain_ref[...]
        nrm[kind * both : (kind + 1) * both, :] = normed.astype(BF16)
        if kind == 0:
            nrm_t[...] = jnp.transpose(normed).astype(BF16)

    acc[...] = jnp.zeros_like(acc)
    sal[...] = jnp.zeros_like(sal)

    def to_right_copy(c):
        return pltpu.make_async_remote_copy(
            src_ref=to_right.at[c], dst_ref=from_left.at[c],
            send_sem=right_send.at[c], recv_sem=right_recv.at[c],
            device_id=at_col(lax.rem(z + 1, cols)), device_id_type=MESH,
        )

    def to_left_copy(c):
        return pltpu.make_async_remote_copy(
            src_ref=to_left.at[c], dst_ref=from_right.at[c],
            send_sem=left_send.at[c], recv_sem=left_recv.at[c],
            device_id=at_col(lax.rem(z + cols - 1, cols)), device_id_type=MESH,
        )

    def make_part(c):
        win_copy(c).wait()
        wout_copy(c).wait()
        part[c, 0 : 2 * both, :] = dot(nrm[...], win[c])
        part[c, 2 * both :, :] = dot(gy[...].reshape(both, width), wout[c], ((1,), (1,)))

    def finish(c):
        total = part[c] + from_left[c].astype(F32) + from_right[c].astype(F32)
        index = dp * nch + c
        pre = total[0 : 2 * both] + bin_ref[pl.ds(index, 1), :]
        cdf = 0.5 * (1.0 + lax.erf(pre * 0.7071067811865476))
        act = pre * cdf
        pre_f = pre[0:both]
        slope = cdf[0:both] + pre_f * jnp.exp(-0.5 * pre_f * pre_f) * 0.3989422804014327
        grad_pre = (total[2 * both :] * slope).astype(BF16)
        act_ft = jnp.transpose(act[0:both]).astype(BF16)
        masked = (act[both:] * keep_ref[pl.ds(index, 1), :]).astype(BF16)
        step = min(width, 512)
        term = jnp.zeros((8, CHUNK), F32)
        lanes_sum = jnp.zeros((CHUNK, 128), F32)
        for k in range(0, width, step):
            span = slice(k, min(k + step, width))
            grad = dot(nrm_t[span, :], grad_pre)
            prod = jnp.abs(win[c, span, :].astype(F32) * grad)
            term = term + jnp.sum(prod.reshape(-1, 8, CHUNK), axis=0)
            grad = dot(act_ft, gy[:, :, span].reshape(both, -1))
            prod = jnp.abs(wout[c, :, span].astype(F32) * grad)
            for q in range(0, prod.shape[1], 128):
                lanes_sum = lanes_sum + prod[:, q : q + 128]
            acc[:, span] += dot(masked, wout[c, :, span])
        total_term = jnp.sum(term, axis=0, keepdims=True) + jnp.sum(
            jnp.transpose(lanes_sum), axis=0, keepdims=True
        )
        sal[pl.ds(c, 1), :] = total_term

    make_part(0)

    def step(s, carry):
        c_right = s - LAG * z
        c_left = s - LAG * (cols - 1 - z)
        c_done = s - LAG * jnp.maximum(z, cols - 1 - z)

        @pl.when((c_right >= 0) & (c_right < nch))
        def _():
            c = c_right

            @pl.when(z > 0)
            def _():
                to_right_copy(c).wait_recv()

            @pl.when(z == 0)
            def _():
                from_left[c] = jnp.zeros(from_left.shape[1:], BF16)

            @pl.when(z < cols - 1)
            def _():
                to_right[c] = (part[c] + from_left[c].astype(F32)).astype(BF16)
                to_right_copy(c).start()

        @pl.when((c_left >= 0) & (c_left < nch))
        def _():
            c = c_left

            @pl.when(z < cols - 1)
            def _():
                to_left_copy(c).wait_recv()

            @pl.when(z == cols - 1)
            def _():
                from_right[c] = jnp.zeros(from_right.shape[1:], BF16)

            @pl.when(z > 0)
            def _():
                to_left[c] = (part[c] + from_right[c].astype(F32)).astype(BF16)
                to_left_copy(c).start()

        @pl.when(s + 1 < nch)
        def _():
            make_part(s + 1)

        @pl.when((c_done >= 0) & (c_done < nch))
        def _():
            finish(c_done)

        return carry

    lax.fori_loop(0, nch + LAG * (cols - 1), step, 0)

    sal_all[z] = sal[...]
    sal_copies = [
        pltpu.make_async_remote_copy(
            src_ref=sal_all.at[z], dst_ref=sal_all.at[z],
            send_sem=sal_send.at[o - 1], recv_sem=sal_recv.at[o - 1],
            device_id=at_col(lax.rem(z + o, cols)), device_id_type=MESH,
        )
        for o in range(1, cols)
    ]
    for copy in sal_copies:
        copy.start()

    half_copy = pltpu.make_async_remote_copy(
        src_ref=acc.at[pl.ds(pl.multiple_of(other * tokens, tokens), tokens), :],
        dst_ref=half, send_sem=half_send, recv_sem=half_recv,
        device_id=at_dp(other), device_id_type=MESH,
    )
    half_copy.start()
    half_copy.wait()
    share = tokens // rows
    here = acc[pl.ds(pl.multiple_of(dp * tokens, tokens), tokens), :] + half[...]
    mine[...] = here.astype(BF16)

    def share_of(r):
        return pl.ds(pl.multiple_of(r * share, share), share)

    blk_copies = [
        pltpu.make_async_remote_copy(
            src_ref=mine.at[share_of(lax.rem(row + o, rows)), :], dst_ref=blocks.at[o - 1],
            send_sem=blk_send.at[o - 1], recv_sem=blk_recv.at[o - 1],
            device_id=at_row(lax.rem(row + o, rows)), device_id_type=MESH,
        )
        for o in range(1, rows)
    ]
    for copy in blk_copies:
        copy.start()

    for copy in sal_copies:
        copy.wait()
    sal_fin[dp] = jnp.sum(sal_all[...], axis=0) * (1.0 / (width * cols))
    fin_copy = pltpu.make_async_remote_copy(
        src_ref=sal_fin.at[dp], dst_ref=sal_fin.at[dp], send_sem=fin_send, recv_sem=fin_recv,
        device_id=at_dp(other), device_id_type=MESH,
    )
    fin_copy.start()

    result = acc[share_of(dp * rows + row), :] + half[share_of(row), :] + bout_ref[...]
    for o, copy in enumerate(blk_copies):
        copy.wait()
        result = result + blocks[o].astype(F32)
    ret_out[...] = result.astype(BF16)
    fin_copy.wait()
    sal_out[...] = sal_fin[...]

    @pl.loop(0, nch)
    def _(c):
        @pl.when(z < cols - 1)
        def _():
            to_right_copy(c).wait_send()

        @pl.when(z > 0)
        def _():
            to_left_copy(c).wait_send()


def local(
    cols, rows,
    forget_tokens, forget_cotangent, forget_labels, retain_tokens, ln_gain,
    w_in, b_in, w_out, b_out, pruned,
):
    tokens, width = forget_tokens.shape
    neurons = w_in.shape[1]
    nch = neurons // 2 // CHUNK
    pad = -(-nch // 8) * 8
    both = 2 * tokens
    grad_y = forget_cotangent * forget_labels[:, None].astype(BF16)
    ids = lax.axis_index("row") * neurons + jnp.arange(neurons, dtype=jnp.int32)
    is_pruned = jnp.any(pruned[:, None] == ids[None, :], axis=0)
    keep = jnp.where(is_pruned, 0.0, 1.0).astype(F32).reshape(2 * nch, CHUNK)
    line = (nch, 3 * both, CHUNK)
    dma = pltpu.SemaphoreType.DMA
    anywhere = pl.BlockSpec(memory_space=pl.ANY)
    vmem = pl.BlockSpec(memory_space=pltpu.VMEM)
    macs = both * width * (neurons // 2) * 6
    saliency, retain_out = pl.pallas_call(
        functools.partial(kernel, (cols, rows, tokens, nch)),
        out_shape=(
            jax.ShapeDtypeStruct((2, pad, CHUNK), F32),
            jax.ShapeDtypeStruct((tokens // rows, width), BF16),
        ),
        in_specs=[anywhere] * 5 + [vmem] * 4,
        out_specs=(vmem, vmem),
        scratch_shapes=[
            pltpu.VMEM((2, 2, tokens, width), BF16),
            pltpu.VMEM((2, tokens, width), BF16),
            pltpu.VMEM((2 * both, width), BF16),
            pltpu.VMEM((width, both), BF16),
            pltpu.VMEM((cols, 8, 2 * both), F32),
            pltpu.VMEM((nch, width, CHUNK), BF16),
            pltpu.VMEM((nch, CHUNK, width), BF16),
            pltpu.VMEM(line, F32),
            pltpu.VMEM(line, BF16),
            pltpu.VMEM(line, BF16),
            pltpu.VMEM(line, BF16),
            pltpu.VMEM(line, BF16),
            pltpu.VMEM((both, width), F32),
            pltpu.VMEM((tokens, width), F32),
            pltpu.VMEM((rows - 1, tokens // rows, width), BF16),
            pltpu.VMEM((tokens, width), BF16),
            pltpu.VMEM((pad, CHUNK), F32),
            pltpu.VMEM((cols, pad, CHUNK), F32),
            pltpu.VMEM((2, pad, CHUNK), F32),
            dma((3,)), dma((3,)), dma((3,)),
            dma((cols - 1,)), dma((cols - 1,)),
            dma((nch,)), dma((nch,)),
            dma((nch,)), dma((nch,)), dma((nch,)), dma((nch,)),
            dma(()), dma(()),
            dma((rows - 1,)), dma((rows - 1,)),
            dma((cols - 1,)), dma((cols - 1,)),
            dma(()), dma(()),
        ],
        compiler_params=pltpu.CompilerParams(
            collective_id=0, has_side_effects=True, vmem_limit_bytes=62 * 2**20
        ),
        cost_estimate=pl.CostEstimate(
            flops=2 * macs, bytes_accessed=2 * width * neurons, transcendentals=0
        ),
        name="unlearn_step",
    )(
        forget_tokens, retain_tokens, grad_y, w_in, w_out,
        ln_gain[None, :], b_in.reshape(2 * nch, CHUNK), keep, b_out[None, :],
    )
    return (saliency[:, :nch].reshape(neurons), retain_out)


def solution(mesh):
    in_specs = (
        P("dp", "col"),
        P("dp", "col"),
        P("dp"),
        P("dp", "col"),
        P("col"),
        P("col", "row"),
        P("row"),
        P("row", "col"),
        P("col"),
        P("row"),
    )
    out_specs = (P("row"), P(("dp", "row"), "col"))
    body = functools.partial(local, mesh.shape["col"], mesh.shape["row"])
    return jax.shard_map(body, mesh=mesh, in_specs=in_specs, out_specs=out_specs, check_vma=False)
```

time: 433 us -> 168 us (0.39)
  waiting for transfers between devices: 273 us -> 0 us
  Pallas kernels: 0 us -> 156 us
  matrix products: 58.5 us -> 0 us
  blocking collectives: 51.3 us -> 0 us
  other arithmetic: 30.6 us -> 3.63 us
  between operations: 14.2 us -> 0.66 us
    reduce_scatter x5 -> x0, waiting for transfers between devices: 185 us -> none  [the longest x1 93.8 us: local(): lax.psum_scatter(partial_pre, 'col', scatter_dimension=1, tiled=True)]
    pallas_call x0 -> x1, Pallas kernels: none -> 156 us  [local(): pl.pallas_call(functools.partial(kernel, (cols, rows, tokens, nch)), out_...]
    all_gather x2 -> x0, waiting for transfers between devices: 87.9 us -> none  [the longest x1 61.3 us: local(): act_all = lax.all_gather(act_share, 'col', axis=1, tiled=True)]
    dot_general x5 -> x0, matrix products: 58.5 us -> none  [the longest x2 19.8 us: outer_rows(): lax.dot_general(left, right, (((0,), (0,)), ((), ())), preferred_element_...]
    psum x3 -> x0, blocking collectives: 51.3 us -> none  [the longest x1 29.5 us: local(): saliency = lax.psum(terms, ('dp', 'col')) / D]
    reduce_sum x4 -> x0, other arithmetic: 22.8 us -> none  [the longest x1 10.5 us: local(): jnp.sum(jnp.abs(weight_in_rows * summed_in), axis=0)]
    convert_element_type x6 -> x1, other arithmetic: 6.61 us -> 0.66 us  [local(): grad_y = forget_cotangent * forget_labels[:, None].astype(BF16)]
  transfers between devices with their start and end apart: 7 -> 0, of which waited for: 7 -> 0; matrix products, arithmetic and copies ran while one was open for 15% -> 0% of each run, Pallas kernels for 0% -> 0%
where the time goes in v1:
time: 168 us; the launch traced here: 167 us
  Pallas kernels  156 us (93%)
  local copies, waits for them, and re-layouts  7.46 us (4%)
  other arithmetic  3.63 us (2%)
    pallas_call x1, Pallas kernels, local(): pl.pallas_call(functools.partial(kernel, (cols, rows, tokens, nch)), out_...  156 us

profile of v1, /device:TPU:0, one launch (start us, length us, event | category | flops | bytes accessed | tf_op | source)
XLA Modules:
  0.0 167.4 jit_solution(11385161979428786942)
XLA Ops:
  0.6 0.7 convert_element_type.4
  1.3 1.3 broadcast_in_dim.17.gain_ref
  2.6 1.3 broadcast_in_dim.20.bout_ref
  3.9 1.1 compare_reduce_fusion
  5.0 0.6 select_n.9.keep_ref
  5.6 1.4 reshape.22.bin_ref
  7.0 1.8 %broadcast_multiply_fusion.gy_hbm = bf16[128,1536]{1,0:T(8,128)(2,1)} fusion(bf16[128,1536]{1,0:T(8,128)(2,1)} %param.11, bf16[128]{0:T(256)(128)(2,1)S(1)} %convert_element_type.4), kind=kLoop, calls=%fused_computation.1 | loop fusion | flops 196608 | bytes 786688 | tf_op jit(solution)/shard_map/mul | solution.py:308
  8.8 155.7 %unlearn_step.1 = (f32[2,16,256]{2,1,0:T(8,128)}, bf16[32,1536]{1,0:T(8,128)(2,1)}) custom-call(bf16[128,1536]{1,0:T(8,128)(2,1)} %ft_hbm.1, bf16[128,1536]{1,0:T(8,128)(2,1)} %rt_hbm.1, bf16[128,1536]{1,0:T(8,128)(2,1)} %broadcast_multiply_fusion.gy_hbm, bf16[1536,6144]{1,0:T(8,128)(2,1)} %win_hbm.1, bf16[6144,1536]{1,0:T(8,128)(2,1)} %wout_hbm.1, ...), custom_call_target="tpu_custom_call" | custom-call | flops 14495514624 | bytes 18874368 | tf_op jit(solution)/shard_map/unlearn_step/pallas_call | solution.py:317
  164.5 1.4 reshape.23
  165.9 1.5 copy.13
  (2 shorter events, 0.0 us)

commit v2 on v1

v2 whole, which is shorter than its diff:
```python
import functools

import jax
import jax.numpy as jnp
from jax import lax
from jax.experimental import pallas as pl
from jax.experimental.pallas import tpu as pltpu
from jax.sharding import PartitionSpec as P

F32, BF16 = jnp.float32, jnp.bfloat16
MESH = pl.DeviceIdType.MESH
CHUNK = 128
SLOTS = 160
LAG = 2


def dot(left, right, contract=((1,), (0,))):
    return lax.dot_general(left, right, (contract, ((), ())), preferred_element_type=F32)


def column(values):
    n = values.shape[1]
    return jnp.transpose(jnp.broadcast_to(values, (128, n)))[:, 0:1]


def prepare(
    sizes,
    ft_hbm, rt_hbm, ct_hbm, lab_ref, gain_ref,
    nrm, nrm_t, gy, count,
    raw, cot, lab, stats,
    raw_loc, raw_send, raw_recv, st_send, st_recv,
):
    cols, tokens = sizes
    width = nrm.shape[1]
    both = 2 * tokens
    dp, row, z = lax.axis_index("dp"), lax.axis_index("row"), lax.axis_index("col")
    other = 1 - dp
    sources = (ft_hbm, rt_hbm, ct_hbm)
    places = (raw.at[0, dp], raw.at[1, dp], cot.at[dp])
    own = [
        pltpu.make_async_copy(src, dst, raw_loc.at[i])
        for i, (src, dst) in enumerate(zip(sources, places))
    ]
    for copy in own:
        copy.start()
    lab[dp] = jnp.broadcast_to(lab_ref[...].astype(F32)[None, :], lab.shape[1:])

    barrier = pltpu.get_barrier_semaphore()
    pl.semaphore_signal(barrier, inc=1, device_id=(other, row, z), device_id_type=MESH)
    for o in range(1, cols):
        pl.semaphore_signal(
            barrier, inc=1, device_id=(dp, row, lax.rem(z + o, cols)), device_id_type=MESH
        )
    pl.semaphore_wait(barrier, cols)

    swaps = [
        pltpu.make_async_remote_copy(
            src_ref=src, dst_ref=dst, send_sem=raw_send.at[i], recv_sem=raw_recv.at[i],
            device_id=(other, row, z), device_id_type=MESH,
        )
        for i, (src, dst) in enumerate(
            zip(sources + (lab.at[dp],), places + (lab.at[dp],))
        )
    ]
    for copy in swaps:
        copy.start()
    for copy in own:
        copy.wait()

    def own_stats(d):
        for kind in range(2):
            x = raw[kind, d].astype(F32)
            mean_here = jnp.sum(x, axis=1, keepdims=True) * (1.0 / width)
            cent = x - mean_here
            square = jnp.sum(cent * cent, axis=1, keepdims=True)
            lane = lax.broadcasted_iota(jnp.int32, (tokens, 128), 1)
            tile = jnp.where(lane == 0, mean_here, square)
            stats[z, 2 * kind + d] = jnp.transpose(tile)[0:8, :]

    own_stats(dp)
    for copy in swaps:
        copy.wait()
    own_stats(other)
    stat_copies = [
        pltpu.make_async_remote_copy(
            src_ref=stats.at[z], dst_ref=stats.at[z],
            send_sem=st_send.at[o - 1], recv_sem=st_recv.at[o - 1],
            device_id=(dp, row, lax.rem(z + o, cols)), device_id_type=MESH,
        )
        for o in range(1, cols)
    ]
    for copy in stat_copies:
        copy.start()

    labels = jnp.concatenate([lab[0][0:1], lab[1][0:1]], axis=1)
    at = lax.broadcasted_iota(jnp.int32, (both, both), 0)
    to = lax.broadcasted_iota(jnp.int32, (both, both), 1)
    until = jnp.where(at <= to, 1.0, 0.0).astype(BF16)
    ranks = dot(jnp.broadcast_to(labels, (16, both)).astype(BF16), until)[0:1]
    spot = jnp.where(labels > 0.5, ranks - 1.0, -1.0)
    select = jnp.where(at.astype(F32) == spot, 1.0, 0.0).astype(BF16)
    count[...] = jnp.broadcast_to(jnp.sum(labels, axis=1, keepdims=True), count.shape)
    gy[...] = dot(select, cot[...].reshape(both, width)).astype(BF16)

    for copy in stat_copies:
        copy.wait()
    gain = gain_ref[...][None, :]
    for kind in range(2):
        scaled = []
        for d in range(2):
            here = stats[:, 2 * kind + d]
            means = here[:, 0:1, :]
            mean_all = jnp.sum(means, axis=0) * (1.0 / cols)
            spread = means - mean_all[None]
            squares = jnp.sum(here[:, 1:2, :] + width * (spread * spread), axis=0)
            scale = lax.rsqrt(squares * (1.0 / (width * cols)) + 1e-06)
            x = raw[kind, d].astype(F32)
            scaled.append(((x - column(mean_all)) * column(scale) * gain).astype(BF16))
        normed = jnp.concatenate(scaled, axis=0)
        if kind == 0:
            chosen = dot(select, normed)
            nrm[0:both, :] = chosen.astype(BF16)
            nrm_t[...] = jnp.transpose(chosen).astype(BF16)
        else:
            nrm[both : 2 * both, :] = normed


def kernel(
    sizes,
    win_hbm, wout_hbm, nrm, nrm_t, gy, bin_ref, pruned_ref, bout_ref,
    sal_out, ret_out,
    win, wout, part, from_left, from_right, to_right, to_left,
    acc, half, blocks, mine, sal, sal_all, sal_fin,
    win_sem, wout_sem,
    right_send, right_recv, left_send, left_recv,
    half_send, half_recv, blk_send, blk_recv, sal_send, sal_recv, fin_send, fin_recv,
):
    cols, rows, tokens, nch, slots = sizes
    width = nrm.shape[1]
    both = 2 * tokens
    dp, row, z = lax.axis_index("dp"), lax.axis_index("row"), lax.axis_index("col")
    other = 1 - dp
    end_f, end_r = slots, slots + both

    def at_dp(d):
        return (d, row, z)

    def at_row(r):
        return (dp, r, z)

    def at_col(c):
        return (dp, row, c)

    def win_copy(c):
        lanes = pl.ds(pl.multiple_of((dp * nch + c) * CHUNK, CHUNK), CHUNK)
        return pltpu.make_async_copy(win_hbm.at[:, lanes], win.at[c], win_sem.at[c])

    def wout_copy(c):
        lines = pl.ds(pl.multiple_of((dp * nch + c) * CHUNK, CHUNK), CHUNK)
        return pltpu.make_async_copy(wout_hbm.at[lines, :], wout.at[c], wout_sem.at[c])

    @pl.loop(0, nch)
    def _(c):
        win_copy(c).start()
        wout_copy(c).start()

    barrier = pltpu.get_barrier_semaphore()
    pl.semaphore_signal(barrier, inc=1, device_id=at_dp(other), device_id_type=MESH)
    for o in range(1, cols):
        pl.semaphore_signal(
            barrier, inc=1, device_id=at_col(lax.rem(z + o, cols)), device_id_type=MESH
        )
    for o in range(1, rows):
        pl.semaphore_signal(
            barrier, inc=1, device_id=at_row(lax.rem(row + o, rows)), device_id_type=MESH
        )
    pl.semaphore_wait(barrier, 1 + (cols - 1) + (rows - 1))

    pruned = column(pruned_ref[...].astype(F32)[None, :])
    lane_ids = lax.broadcasted_iota(jnp.int32, (1, CHUNK), 1)
    acc[...] = jnp.zeros_like(acc)
    sal[...] = jnp.zeros_like(sal)

    def to_right_copy(c):
        return pltpu.make_async_remote_copy(
            src_ref=to_right.at[c], dst_ref=from_left.at[c],
            send_sem=right_send.at[c], recv_sem=right_recv.at[c],
            device_id=at_col(lax.rem(z + 1, cols)), device_id_type=MESH,
        )

    def to_left_copy(c):
        return pltpu.make_async_remote_copy(
            src_ref=to_left.at[c], dst_ref=from_right.at[c],
            send_sem=left_send.at[c], recv_sem=left_recv.at[c],
            device_id=at_col(lax.rem(z + cols - 1, cols)), device_id_type=MESH,
        )

    def make_part(c):
        win_copy(c).wait()
        wout_copy(c).wait()
        part[c, 0:end_f, :] = dot(nrm[0:slots, :], win[c])
        part[c, end_f:end_r, :] = dot(nrm[both : 2 * both, :], win[c])
        part[c, end_r:, :] = dot(gy[0:slots, :], wout[c], ((1,), (1,)))

    def finish(c):
        total = part[c] + from_left[c].astype(F32) + from_right[c].astype(F32)
        first = pl.multiple_of((dp * nch + c) * CHUNK, CHUNK)
        pre = total[0:end_r] + bin_ref[pl.ds(first, CHUNK)][None, :]
        cdf = 0.5 * (1.0 + lax.erf(pre * 0.7071067811865476))
        act = pre * cdf
        pre_f = pre[0:slots]
        slope = cdf[0:slots] + pre_f * jnp.exp(-0.5 * pre_f * pre_f) * 0.3989422804014327
        grad_pre, act_f = total[end_r:] * slope, act[0:slots]
        if slots < both:
            rest = jnp.zeros((both - slots, CHUNK), F32)
            grad_pre = jnp.concatenate([grad_pre, rest], axis=0)
            act_f = jnp.concatenate([act_f, rest], axis=0)
        grad_pre = grad_pre.astype(BF16)
        act_ft = jnp.transpose(act_f).astype(BF16)
        ids = (lane_ids + (row * (2 * nch * CHUNK) + first)).astype(F32)
        hits = jnp.max(jnp.where(pruned == ids, 1.0, 0.0), axis=0, keepdims=True)
        masked = (act[slots:] * (1.0 - hits)).astype(BF16)
        step = min(width, 512)
        term = jnp.zeros((8, CHUNK), F32)
        lanes_sum = jnp.zeros((CHUNK, 128), F32)
        for k in range(0, width, step):
            span = slice(k, min(k + step, width))
            grad = dot(nrm_t[span, :], grad_pre)
            prod = jnp.abs(win[c, span, :].astype(F32) * grad)
            term = term + jnp.sum(prod.reshape(-1, 8, CHUNK), axis=0)
            grad = dot(act_ft, gy[:, span])
            prod = jnp.abs(wout[c, :, span].astype(F32) * grad)
            for q in range(0, prod.shape[1], 128):
                lanes_sum = lanes_sum + prod[:, q : q + 128]
            acc[:, span] += dot(masked, wout[c, :, span])
        total_term = jnp.sum(term, axis=0, keepdims=True) + jnp.sum(
            jnp.transpose(lanes_sum), axis=0, keepdims=True
        )
        sal[pl.ds(c, 1), :] = total_term

    make_part(0)

    def step(s, carry):
        c_right = s - LAG * z
        c_left = s - LAG * (cols - 1 - z)
        c_done = s - LAG * jnp.maximum(z, cols - 1 - z)

        @pl.when((c_right >= 0) & (c_right < nch))
        def _():
            c = c_right

            @pl.when(z > 0)
            def _():
                to_right_copy(c).wait_recv()

            @pl.when(z == 0)
            def _():
                from_left[c] = jnp.zeros(from_left.shape[1:], BF16)

            @pl.when(z < cols - 1)
            def _():
                to_right[c] = (part[c] + from_left[c].astype(F32)).astype(BF16)
                to_right_copy(c).start()

        @pl.when((c_left >= 0) & (c_left < nch))
        def _():
            c = c_left

            @pl.when(z < cols - 1)
            def _():
                to_left_copy(c).wait_recv()

            @pl.when(z == cols - 1)
            def _():
                from_right[c] = jnp.zeros(from_right.shape[1:], BF16)

            @pl.when(z > 0)
            def _():
                to_left[c] = (part[c] + from_right[c].astype(F32)).astype(BF16)
                to_left_copy(c).start()

        @pl.when(s + 1 < nch)
        def _():
            make_part(s + 1)

        @pl.when((c_done >= 0) & (c_done < nch))
        def _():
            finish(c_done)

        return carry

    lax.fori_loop(0, nch + LAG * (cols - 1), step, 0)

    sal_all[z] = sal[...]
    sal_copies = [
        pltpu.make_async_remote_copy(
            src_ref=sal_all.at[z], dst_ref=sal_all.at[z],
            send_sem=sal_send.at[o - 1], recv_sem=sal_recv.at[o - 1],
            device_id=at_col(lax.rem(z + o, cols)), device_id_type=MESH,
        )
        for o in range(1, cols)
    ]
    for copy in sal_copies:
        copy.start()

    half_copy = pltpu.make_async_remote_copy(
        src_ref=acc.at[pl.ds(pl.multiple_of(other * tokens, tokens), tokens), :],
        dst_ref=half, send_sem=half_send, recv_sem=half_recv,
        device_id=at_dp(other), device_id_type=MESH,
    )
    half_copy.start()
    half_copy.wait()
    share = tokens // rows
    here = acc[pl.ds(pl.multiple_of(dp * tokens, tokens), tokens), :] + half[...]
    mine[...] = here.astype(BF16)

    def share_of(r):
        return pl.ds(pl.multiple_of(r * share, share), share)

    blk_copies = [
        pltpu.make_async_remote_copy(
            src_ref=mine.at[share_of(lax.rem(row + o, rows)), :], dst_ref=blocks.at[o - 1],
            send_sem=blk_send.at[o - 1], recv_sem=blk_recv.at[o - 1],
            device_id=at_row(lax.rem(row + o, rows)), device_id_type=MESH,
        )
        for o in range(1, rows)
    ]
    for copy in blk_copies:
        copy.start()

    for copy in sal_copies:
        copy.wait()
    sal_fin[dp] = jnp.sum(sal_all[...], axis=0) * (1.0 / (width * cols))
    fin_copy = pltpu.make_async_remote_copy(
        src_ref=sal_fin.at[dp], dst_ref=sal_fin.at[dp], send_sem=fin_send, recv_sem=fin_recv,
        device_id=at_dp(other), device_id_type=MESH,
    )
    fin_copy.start()

    result = acc[share_of(dp * rows + row), :] + half[share_of(row), :] + bout_ref[...][None, :]
    for o, copy in enumerate(blk_copies):
        copy.wait()
        result = result + blocks[o].astype(F32)
    ret_out[...] = result.astype(BF16)
    fin_copy.wait()
    sal_out[...] = sal_fin[...]

    @pl.loop(0, nch)
    def _(c):
        @pl.when(z < cols - 1)
        def _():
            to_right_copy(c).wait_send()

        @pl.when(z > 0)
        def _():
            to_left_copy(c).wait_send()


def local(
    cols, rows,
    forget_tokens, forget_cotangent, forget_labels, retain_tokens, ln_gain,
    w_in, b_in, w_out, b_out, pruned,
):
    tokens, width = forget_tokens.shape
    neurons = w_in.shape[1]
    nch = neurons // 2 // CHUNK
    pad = -(-nch // 8) * 8
    both = 2 * tokens
    dma = pltpu.SemaphoreType.DMA
    anywhere = pl.BlockSpec(memory_space=pl.ANY)
    vmem = pl.BlockSpec(memory_space=pltpu.VMEM)
    nrm, nrm_t, gy, count = pl.pallas_call(
        functools.partial(prepare, (cols, tokens)),
        out_shape=(
            jax.ShapeDtypeStruct((2 * both, width), BF16),
            jax.ShapeDtypeStruct((width, both), BF16),
            jax.ShapeDtypeStruct((both, width), BF16),
            jax.ShapeDtypeStruct((8, 128), F32),
        ),
        in_specs=[anywhere] * 3 + [vmem] * 2,
        out_specs=(vmem,) * 4,
        scratch_shapes=[
            pltpu.VMEM((2, 2, tokens, width), BF16),
            pltpu.VMEM((2, tokens, width), BF16),
            pltpu.VMEM((2, 8, tokens), F32),
            pltpu.VMEM((cols, 4, 8, tokens), F32),
            dma((3,)), dma((4,)), dma((4,)),
            dma((cols - 1,)), dma((cols - 1,)),
        ],
        compiler_params=pltpu.CompilerParams(
            collective_id=0, has_side_effects=True, vmem_limit_bytes=62 * 2**20
        ),
        name="prepare",
    )(forget_tokens, retain_tokens, forget_cotangent, forget_labels, ln_gain)

    def stream(slots, collective_id):
        line = (nch, 2 * slots + both, CHUNK)
        macs = 3 * (slots + both) * width * (neurons // 2)
        return pl.pallas_call(
            functools.partial(kernel, (cols, rows, tokens, nch, slots)),
            out_shape=(
                jax.ShapeDtypeStruct((2, pad, CHUNK), F32),
                jax.ShapeDtypeStruct((tokens // rows, width), BF16),
            ),
            in_specs=[anywhere] * 2 + [vmem] * 6,
            out_specs=(vmem, vmem),
            scratch_shapes=[
                pltpu.VMEM((nch, width, CHUNK), BF16),
                pltpu.VMEM((nch, CHUNK, width), BF16),
                pltpu.VMEM(line, F32),
                pltpu.VMEM(line, BF16),
                pltpu.VMEM(line, BF16),
                pltpu.VMEM(line, BF16),
                pltpu.VMEM(line, BF16),
                pltpu.VMEM((both, width), F32),
                pltpu.VMEM((tokens, width), F32),
                pltpu.VMEM((rows - 1, tokens // rows, width), BF16),
                pltpu.VMEM((tokens, width), BF16),
                pltpu.VMEM((pad, CHUNK), F32),
                pltpu.VMEM((cols, pad, CHUNK), F32),
                pltpu.VMEM((2, pad, CHUNK), F32),
                dma((nch,)), dma((nch,)),
                dma((nch,)), dma((nch,)), dma((nch,)), dma((nch,)),
                dma(()), dma(()),
                dma((rows - 1,)), dma((rows - 1,)),
                dma((cols - 1,)), dma((cols - 1,)),
                dma(()), dma(()),
            ],
            compiler_params=pltpu.CompilerParams(
                collective_id=collective_id, has_side_effects=True, vmem_limit_bytes=62 * 2**20
            ),
            cost_estimate=pl.CostEstimate(
                flops=2 * macs, bytes_accessed=2 * width * neurons, transcendentals=0
            ),
            name="stream_%d" % slots,
        )

    rest = (w_in, w_out, nrm, nrm_t, gy, b_in, pruned, b_out)
    few = SLOTS * both // 256
    saliency, retain_out = lax.cond(
        count[0, 0] <= few,
        lambda args: tuple(stream(few, 1)(*args)),
        lambda args: tuple(stream(both, 2)(*args)),
        rest,
    )
    return (saliency[:, :nch].reshape(neurons), retain_out)


def solution(mesh):
    in_specs = (
        P("dp", "col"),
        P("dp", "col"),
        P("dp"),
        P("dp", "col"),
        P("col"),
        P("col", "row"),
        P("row"),
        P("row", "col"),
        P("col"),
        P("row"),
    )
    out_specs = (P("row"), P(("dp", "row"), "col"))
    body = functools.partial(local, mesh.shape["col"], mesh.shape["row"])
    return jax.shard_map(body, mesh=mesh, in_specs=in_specs, out_specs=out_specs, check_vma=False)
```

time: 168 us -> 124 us (0.74)
  Pallas kernels: 156 us -> 120 us
  local copies, waits for them, and re-layouts: 7.46 us -> 2.44 us
  other arithmetic: 3.63 us -> 0 us
    pallas_call x1 -> x2, Pallas kernels: 156 us -> 120 us  [the longest x1 106 us: local(): stream(few, 1)(*args)]
    reshape x2 -> x0, local copies, waits for them, and re-layouts: 2.72 us -> none  [the longest x1 1.37 us: local(): return (saliency[:, :nch].reshape(neurons), retain_out)]
    broadcast_in_dim x2 -> x0, local copies, waits for them, and re-layouts: 2.59 us -> none  [the longest x1 1.29 us: local(): b_out[None, :]]
    mul x1 -> x0, other arithmetic: 1.83 us -> none  [local(): grad_y = forget_cotangent * forget_labels[:, None].astype(BF16)]
where the time goes in v2:
time: 124 us
  Pallas kernels  120 us (97%)
  local copies, waits for them, and re-layouts  2.44 us (2%)
  between operations  1.3 us (1%)
    pallas_call x1, Pallas kernels, local(): stream(few, 1)(*args)  106 us
    pallas_call x1, Pallas kernels, local(): pl.pallas_call(functools.partial(prepare, (cols, tokens)), out_shape=(jax...  13.8 us

profile of v2, /device:TPU:0, one launch (start us, length us, event | category | flops | bytes accessed | tf_op | source)
XLA Modules:
  0.0 123.7 jit_solution(2822065670273842187)
XLA Ops:
  0.6 13.8 %prepare.1 = (bf16[512,1536]{1,0:T(8,128)(2,1)S(1)}, bf16[1536,256]{1,0:T(8,128)(2,1)}, bf16[256,1536]{1,0:T(8,128)(2,1)}, f32[8,128]{1,0:T(8,128)}) custom-call(bf16[128,1536]{1,0:T(8,128)(2,1)} %ft_hbm.1, bf16[128,1536]{1,0:T(8,128)(2,1)} %rt_hbm.1, bf16[128,1536]{1,0:T(8,128)(2,1)} %ct_hbm.1, s32[128]{0:T(128)} %lab_ref.1, f32[1536]{0:T(1024)} %gain_ref.1), custom_call_target="tpu_custom_call" | custom-call | tf_op jit(solution)/shard_map/prepare/pallas_call | solution.py:372
  14.4 1.2 slice.3
  16.3 106.2 %conditional.1 = (bf16[32,1536]{1,0:T(8,128)(2,1)S(1)}, f32[6144]{0:T(1024)S(1)}) conditional(s32[]{:T(128)} %bitcast.2, (bf16[1536,6144]{1,0:T(8,128)(2,1)}, bf16[6144,1536]{1,0:T(8,128)(2,1)}, bf16[512,1536]{1,0:T(8,128)(2,1)S(1)}, bf16[1536,256]{1,0:T(8,128)(2,1)}, bf16[256,1536]{1,0:T(8,128)(2,1)}, /*index=5*/f32[6144]{0:T(1024)}, s32[128]{0:T(128)}, ...), branch_computations={%region_0.0_spmd, %region_1.0_spmd} | conditional | flops 14495514624 | bytes 18874384 | solution.py:440
  16.3 106.2 %stream_160.1 = (f32[2,24,128]{2,1,0:T(8,128)S(1)}, bf16[32,1536]{1,0:T(8,128)(2,1)S(1)}) custom-call(bf16[1536,6144]{1,0:T(8,128)(2,1)} %get-tuple-element.47.win_hbm, bf16[6144,1536]{1,0:T(8,128)(2,1)} %get-tuple-element.48.wout_hbm, bf16[512,1536]{1,0:T(8,128)(2,1)S(1)} %get-tuple-element.49.nrm, bf16[1536,256]{1,0:T(8,128)(2,1)} %get-tuple-element.50.nrm_t, ...), custom_call_target="tpu_custom_call" | custom-call | flops 11777605632 | bytes 18874368 | tf_op jit(solution)/shard_map/cond/branch_1_fun/stream_160/pallas_call | solution.py:442
  122.4 0.6 copy.18
  123.0 0.6 copy.19
